TPU v7x, 256 devices: a whole 4x4x8 slice. The times are simulated.
256 devices in a mesh: dp: 8 (over x, y_hi), pencil: 32 (over z, y_lo, core).
Axes of the slice: x: 4, y: 4 (y_hi: 2, y_lo: 2; y = y_hi * 2 + y_lo), z: 8, core: 2. Of those that a mesh axis runs over, the one named last changes fastest.
Arguments:
- fields: bfloat16 [8, 256, 32, 4096], P('dp', 'pencil'), may hold values from -6 to 6
- cotangent: bfloat16 [8, 256, 32, 4096], P('dp', 'pencil'), may hold values from -6 to 6
- spectral_weight: bfloat16 [32, 2, 512, 1024], P(None, None, 'pencil'), may hold values from -4 to 4
Outputs:
- grad_fields: bfloat16 [8, 256, 32, 4096], P('dp', 'pencil')
- grad_weight: float32 [32, 2, 512, 1024], P('dp', None, 'pencil')
All inputs are finite; a program needn't handle non-finite values.
Results may differ from a plain program's by a relative error of at most 0.023.
Values may be sent and summed in bfloat16 or wider, within the bound.
A program may use at most 128 MiB of HBM per device.

v0:
```python
import functools
import math

import jax
import jax.numpy as jnp
import numpy as np
from jax import lax
from jax.experimental import pallas as pl
from jax.experimental.pallas import tpu as pltpu
from jax.sharding import PartitionSpec as P

C = 32
MX = 32
MY = 32
MZ = 16
NX = 256
NY = 128
NZ = 32
PLANE = NY * NZ
PENCIL = 32
GROUPS = 8
XD = NX // PENCIL
ROWS = XD * C
SPEC = PENCIL * 2 * MZ
HALF = 128
CHUNKS = 4
MESH = pl.DeviceIdType.MESH
F32 = jnp.float32
BF16 = jnp.bfloat16

ERFCX = (
    0.1396285169187187,
    0.13968893082035916,
    0.12150772849569927,
    0.09702409559327627,
    0.001681622922537982,
    0.11598743251926187,
    -0.21153701193576485,
    0.11952101759674227,
    -0.02350221617294912,
)
DENSITY = 0.3989422804014327


def gelu_slope(v):
    a = jnp.abs(v)
    t = 1.0 / (1.0 + 0.35 * a)
    q = jnp.full_like(t, ERFCX[-1])
    for coef in ERFCX[-2::-1]:
        q = q * t + coef
    h = jnp.exp(-0.5 * v * v) * (q * t - DENSITY * a)
    return jnp.where(v >= 0.0, 1.0 - h, h)


@functools.lru_cache(None)
def tables():
    b = np.arange(MY)[:, None, None]
    c = np.arange(MZ)[None, :, None]
    p = np.arange(PLANE)[None, None, :]
    y, z = p % NY, p // NY
    turns = ((b - MY // 2) * y * (NZ // 1) + c * z * NY) % (NY * NZ)
    angle = turns * (2.0 * math.pi / (NY * NZ))
    plane = np.stack([np.cos(angle), -np.sin(angle)], axis=1).reshape(SPEC, PLANE)
    kx = np.arange(MX)[:, None] - MX // 2
    j = np.arange(ROWS)[None, :] // C
    phase = ((kx * j) % NX) * (2.0 * math.pi / NX)
    twiddle = np.stack([np.cos(phase), np.sin(phase)], axis=1)
    spread = np.zeros((HALF, C * C))
    spread[np.arange(C * C) // C, np.arange(C * C)] = 1.0
    gather = np.zeros((C * C, HALF))
    lane = np.arange(HALF)
    gather[:] = (np.arange(C * C)[:, None] // C) == (lane[None, :] % C)
    return (
        plane.astype(jnp.bfloat16),
        twiddle.astype(np.float32),
        spread.astype(jnp.bfloat16),
        gather.astype(jnp.bfloat16),
    )


def times(value, angle, sign):
    re, im = value
    if angle == 0:
        return value
    co, si = math.cos(2 * math.pi * angle), sign * math.sin(2 * math.pi * angle)
    if angle in (0.125, 0.375):
        root = math.sqrt(0.5)
        if angle == 0.125:
            if sign > 0:
                return (re - im) * root, (re + im) * root
            return (re + im) * root, (im - re) * root
        if sign > 0:
            return (re + im) * (-root), (re - im) * root
        return (im - re) * root, (re + im) * (-root)
    return re * co - im * si, re * si + im * co


def add(a, b):
    return a[0] + b[0], a[1] + b[1]


def sub(a, b):
    return a[0] - b[0], a[1] - b[1]


def fft(values, sign):
    n = len(values)
    if n == 1:
        return values
    even, odd = fft(values[0::2], sign), fft(values[1::2], sign)
    out = [None] * n
    for k in range(n // 2):
        if k * 4 == n:
            re, im = odd[k]
            turned = (-im, re) if sign > 0 else (im, -re)
        else:
            turned = times(odd[k], k / n, sign)
        out[k] = add(even[k], turned)
        out[k + n // 2] = sub(even[k], turned)
    return out


def dot(a, b, dims):
    return lax.dot_general(a, b, (dims, ((), ())), preferred_element_type=F32)


def kernel(
    x_hbm, cot_hbm, w_hbm, table_hbm, tw_ref, spread_ref, gather_ref,
    out_hbm, gw_hbm,
    x_ref, cot_ref, w_ref, table, send, recv, spec, grad, mixed, terms, acc, dx, dg, out_ref, gw_ref,
    load_sem, own_sem, send_sem, recv_sem, dp_send, dp_recv, dp_own, store_sem,
):
    me = lax.axis_index("pencil")
    group = lax.axis_index("dp")

    load_x = pltpu.make_async_copy(x_hbm, x_ref, load_sem.at[0])
    load_cot = pltpu.make_async_copy(cot_hbm, cot_ref, load_sem.at[1])
    load_w = pltpu.make_async_copy(w_hbm, w_ref, load_sem.at[2])
    chunk_rows = SPEC // CHUNKS
    chunk_peers = PENCIL // CHUNKS

    def chunk_of(step):
        return lax.rem(me // chunk_peers + step, CHUNKS)

    def load_table(step):
        rows = pl.ds(pl.multiple_of(chunk_of(step) * chunk_rows, chunk_rows), chunk_rows)
        return pltpu.make_async_copy(table_hbm.at[rows], table.at[rows], load_sem.at[3 + step])

    load_x.start()
    for step in range(CHUNKS):
        load_table(step).start()
    load_cot.start()
    load_w.start()

    barrier = pltpu.get_barrier_semaphore()

    def greet_pencil(i, carry):
        pl.semaphore_signal(
            barrier, inc=1, device_id=(group, lax.rem(me + i, PENCIL)), device_id_type=MESH
        )
        return carry

    def greet_group(i, carry):
        pl.semaphore_signal(
            barrier, inc=1, device_id=(lax.rem(group + i, GROUPS), me), device_id_type=MESH
        )
        return carry

    lax.fori_loop(1, PENCIL, greet_pencil, 0)
    lax.fori_loop(1, GROUPS, greet_group, 0)

    def post(phase, half, peer):
        pltpu.make_async_remote_copy(
            src_ref=send.at[phase, half, peer],
            dst_ref=recv.at[phase, half, me],
            send_sem=send_sem.at[phase, half],
            recv_sem=recv_sem.at[phase, half],
            device_id=(group, peer),
            device_id_type=MESH,
        ).start()

    def own_copy(phase, half):
        return pltpu.make_async_copy(
            send.at[phase, half, me], recv.at[phase, half, me], own_sem.at[phase, half]
        )

    def arrived(phase, half):
        block = recv.at[phase, half, pl.ds(0, PENCIL - 1)]
        pltpu.make_async_copy(block, block, recv_sem.at[phase, half]).wait()
        own_copy(phase, half).wait()

    def sent(phase, half):
        block = send.at[phase, half, pl.ds(0, PENCIL - 1)]
        pltpu.make_async_copy(block, block, send_sem.at[phase, half]).wait()

    def post_all(phase, half):
        def one(i, carry):
            post(phase, half, lax.rem(me + i, PENCIL))
            return carry

        lax.fori_loop(1, PENCIL, one, 0)
        own_copy(phase, half).start()

    def post_chunk(phase, half, chunk):
        def one(i, carry):
            peer = chunk * chunk_peers + lax.rem(me + i, chunk_peers)

            @pl.when(peer != me)
            def _():
                post(phase, half, peer)

            return carry

        lax.fori_loop(0, chunk_peers, one, 0)

    def plane_forward_chunk(source, phase, halves, chunk):
        rows = pl.ds(pl.multiple_of(chunk * chunk_rows, chunk_rows), chunk_rows)
        result = dot(table[rows, :], source, ((1,), (1,))).astype(BF16)
        for place, half in enumerate(halves):
            part = result[:, place * HALF : (place + 1) * HALF]
            send[phase, half, pl.ds(chunk * chunk_peers, chunk_peers)] = part.reshape(
                chunk_peers, 2, MZ, HALF
            )

    def first_forward(phase, half, scale, target):
        values = [
            (recv[phase, half, d, 0].astype(F32), recv[phase, half, d, 1].astype(F32))
            for d in range(PENCIL)
        ]
        spectrum = fft(values, -1)
        for a in range(MX):
            re, im = spectrum[(a - MX // 2) % MX]
            co = tw_ref[a, 0:1, half * HALF : (half + 1) * HALF]
            si = tw_ref[a, 1:2, half * HALF : (half + 1) * HALF]
            parts = (re * co + im * si, im * co - re * si)
            for r in range(2):
                if half == 0:
                    acc[a, r] = parts[r]
                else:
                    total = acc[a, r] + parts[r]
                    total = total + pltpu.roll(total, 64, 1)
                    total = total + pltpu.roll(total, 32, 1)
                    if scale is not None:
                        total = total * scale
                    target[a, r] = total.astype(BF16)

    def first_inverse(phase, half, scale):
        values = [None] * MX
        for a in range(MX):
            re, im = mixed[a, 0], mixed[a, 1]
            co = tw_ref[a, 0:1, half * HALF : (half + 1) * HALF]
            si = tw_ref[a, 1:2, half * HALF : (half + 1) * HALF]
            values[(a - MX // 2) % MX] = (re * co - im * si, im * co + re * si)
        signal = fft(values, 1)
        for d in range(PENCIL):
            for r in range(2):
                value = signal[d][r]
                if scale is not None:
                    value = value * scale
                send[phase, half, d, r] = value.astype(BF16)

    def share(source, target, which):
        def one(i, carry):
            peer = lax.rem(group + i, GROUPS)
            pltpu.make_async_remote_copy(
                src_ref=source.at[pl.ds(peer * (MX // GROUPS), MX // GROUPS)],
                dst_ref=target.at[group],
                send_sem=dp_send.at[which],
                recv_sem=dp_recv.at[which],
                device_id=(peer, me),
                device_id_type=MESH,
            ).start()
            return carry

        lax.fori_loop(1, GROUPS, one, 0)
        share_own(source, target, which).start()

    def share_own(source, target, which):
        return pltpu.make_async_copy(
            source.at[pl.ds(group * (MX // GROUPS), MX // GROUPS)],
            target.at[group],
            dp_own.at[which],
        )

    def shared(source, target, which):
        block = target.at[pl.ds(0, GROUPS - 1)]
        pltpu.make_async_copy(block, block, dp_recv.at[which]).wait()
        pltpu.make_async_copy(block, block, dp_send.at[which]).wait()
        share_own(source, target, which).wait()

    depth = lax.broadcasted_iota(jnp.int32, (MZ, HALF), 0)
    mode_scale = jnp.where(depth == 0, 1.0, 2.0).astype(F32) * (1.0 / (NX * NY * NZ))

    load_x.wait()
    for step in range(CHUNKS):
        load_table(step).wait()
        chunk = chunk_of(step)
        plane_forward_chunk(x_ref[...], 0, (0, 1), chunk)
        if step == 0:
            pl.semaphore_wait(barrier, PENCIL + GROUPS - 2)
        for half in range(2):
            post_chunk(0, half, chunk)
    for half in range(2):
        own_copy(0, half).start()
    load_w.wait()
    load_cot.wait()
    for half in range(2):
        arrived(0, half)
        first_forward(0, half, None, spec)
    share(spec, dx, 0)

    block_a = 4

    def forward_mix(step, carry):
        a0 = step * block_a
        lines = spec[pl.ds(a0, block_a)].reshape(block_a * 2 * MZ, HALF)
        wide = dot(lines, spread_ref[...], ((1,), (0,))).reshape(block_a, 2, MZ, C * C)
        for a in range(block_a):
            out_re = jnp.zeros((MZ, HALF), F32)
            out_im = jnp.zeros((MZ, HALF), F32)
            for t in range(C * C // HALF):
                lanes = slice(t * HALF, (t + 1) * HALF)
                w_re = w_ref[a0 + a, 0, :, lanes].astype(F32)
                w_im = w_ref[a0 + a, 1, :, lanes].astype(F32)
                x_re, x_im = wide[a, 0, :, lanes], wide[a, 1, :, lanes]
                out_re = out_re + x_re * w_re - x_im * w_im
                out_im = out_im + x_re * w_im + x_im * w_re
            for r, total in enumerate((out_re, out_im)):
                total = total + pltpu.roll(total, 64, 1)
                total = total + pltpu.roll(total, 32, 1)
                mixed[a0 + a, r] = total.astype(BF16).astype(F32)
        return carry

    lax.fori_loop(0, MX // block_a, forward_mix, 0)

    for half in range(2):
        first_inverse(1, half, mode_scale)
        post_all(1, half)

    width = 512
    for half in range(2):
        arrived(1, half)
        lines = recv[1, half].reshape(SPEC, HALF).T
        rows = pl.ds(half * HALF, HALF)

        def cells(step, carry):
            lanes = pl.ds(pl.multiple_of(step * width, width), width)
            pre = dot(lines, table[:, lanes], ((1,), (0,)))
            slope = gelu_slope(pre) * cot_ref[rows, lanes].astype(F32)
            grad[rows, lanes] = slope.astype(BF16)
            return carry

        lax.fori_loop(0, PLANE // width, cells, 0)
        for step in range(CHUNKS):
            chunk = chunk_of(step)
            plane_forward_chunk(grad[rows, :], 2, (half,), chunk)
            post_chunk(2, half, chunk)
        own_copy(2, half).start()

    for half in range(2):
        arrived(2, half)
        first_forward(2, half, mode_scale, terms)
    share(terms, dg, 1)

    def backward_mix(step, carry):
        a0 = step * block_a
        for a in range(block_a):
            g_re, g_im = terms[a0 + a, 0].astype(F32), terms[a0 + a, 1].astype(F32)
            parts_re, parts_im = [], []
            for t in range(C * C // HALF):
                lanes = slice(t * HALF, (t + 1) * HALF)
                w_re = w_ref[a0 + a, 0, :, lanes].astype(F32)
                w_im = w_ref[a0 + a, 1, :, lanes].astype(F32)
                parts_re.append((g_re * w_re + g_im * w_im).astype(BF16))
                parts_im.append((g_im * w_re - g_re * w_im).astype(BF16))
            both = jnp.concatenate(
                [jnp.concatenate(parts_re, axis=1), jnp.concatenate(parts_im, axis=1)], axis=0
            )
            sums = dot(both, gather_ref[...], ((1,), (0,))).astype(BF16).astype(F32)
            mixed[a0 + a] = sums.reshape(2, MZ, HALF)
        return carry

    lax.fori_loop(0, MX // block_a, backward_mix, 0)

    for half in range(2):
        first_inverse(3, half, None)
        post_all(3, half)

    shared(spec, dx, 0)
    shared(terms, dg, 1)

    def outer(a, carry):
        lines = jnp.concatenate([dx[s, a].reshape(2 * MZ, HALF) for s in range(GROUPS)], axis=0)
        wide = dot(lines, spread_ref[...], ((1,), (0,))).reshape(GROUPS, 2, MZ, C * C)
        g = [(dg[s, a, 0].astype(F32), dg[s, a, 1].astype(F32)) for s in range(GROUPS)]
        for t in range(C * C // HALF):
            lanes = slice(t * HALF, (t + 1) * HALF)
            out_re = jnp.zeros((MZ, HALF), F32)
            out_im = jnp.zeros((MZ, HALF), F32)
            for s in range(GROUPS):
                x_re, x_im = wide[s, 0, :, lanes], wide[s, 1, :, lanes]
                out_re = out_re + x_re * g[s][0] + x_im * g[s][1]
                out_im = out_im + x_re * g[s][1] - x_im * g[s][0]
            gw_ref[a, 0, :, lanes] = out_re
            gw_ref[a, 1, :, lanes] = out_im
        return carry

    lax.fori_loop(0, MX // GROUPS, outer, 0)
    store_gw = pltpu.make_async_copy(gw_ref, gw_hbm, store_sem.at[2])
    store_gw.start()

    for half in range(2):
        arrived(3, half)
        lines = recv[3, half].reshape(SPEC, HALF).T
        rows = pl.ds(half * HALF, HALF)

        def finish(step, carry):
            lanes = pl.ds(pl.multiple_of(step * width, width), width)
            out_ref[rows, lanes] = dot(lines, table[:, lanes], ((1,), (0,))).astype(BF16)
            return carry

        lax.fori_loop(0, PLANE // width, finish, 0)
        pltpu.make_async_copy(out_ref.at[rows], out_hbm.at[rows], store_sem.at[half]).start()

    for phase in range(4):
        for half in range(2):
            sent(phase, half)
    for half in range(2):
        rows = pl.ds(half * HALF, HALF)
        pltpu.make_async_copy(out_ref.at[rows], out_hbm.at[rows], store_sem.at[half]).wait()
    store_gw.wait()


def per_device(fields, cotangent, spectral_weight):
    plane, twiddle, spread, gather = tables()
    any_space = pl.BlockSpec(memory_space=pl.ANY)
    vmem = pl.BlockSpec(memory_space=pltpu.VMEM)
    block = (PENCIL, 2, MZ, HALF)
    spectrum = (MX, 2, MZ, HALF)
    mine = MX // GROUPS
    grad_fields, grad_weight = pl.pallas_call(
        kernel,
        out_shape=(
            jax.ShapeDtypeStruct((ROWS, PLANE), BF16),
            jax.ShapeDtypeStruct((mine, 2, MZ, C * C), F32),
        ),
        in_specs=[any_space] * 4 + [vmem] * 3,
        out_specs=(any_space, any_space),
        scratch_shapes=[
            pltpu.VMEM((ROWS, PLANE), BF16),
            pltpu.VMEM((ROWS, PLANE), BF16),
            pltpu.VMEM((MX, 2, MZ, C * C), BF16),
            pltpu.VMEM((SPEC, PLANE), BF16),
            pltpu.VMEM((4, 2) + block, BF16),
            pltpu.VMEM((4, 2) + block, BF16),
            pltpu.VMEM(spectrum, BF16),
            pltpu.VMEM((ROWS, PLANE), BF16),
            pltpu.VMEM(spectrum, F32),
            pltpu.VMEM(spectrum, BF16),
            pltpu.VMEM(spectrum, F32),
            pltpu.VMEM((GROUPS, mine, 2, MZ, HALF), BF16),
            pltpu.VMEM((GROUPS, mine, 2, MZ, HALF), BF16),
            pltpu.VMEM((ROWS, PLANE), BF16),
            pltpu.VMEM((mine, 2, MZ, C * C), F32),
            pltpu.SemaphoreType.DMA((3 + CHUNKS,)),
            pltpu.SemaphoreType.DMA((4, 2)),
            pltpu.SemaphoreType.DMA((4, 2)),
            pltpu.SemaphoreType.DMA((4, 2)),
            pltpu.SemaphoreType.DMA((2,)),
            pltpu.SemaphoreType.DMA((2,)),
            pltpu.SemaphoreType.DMA((2,)),
            pltpu.SemaphoreType.DMA((3,)),
        ],
        compiler_params=pltpu.CompilerParams(
            collective_id=0, has_side_effects=True, vmem_limit_bytes=56 * 2**20
        ),
        cost_estimate=pl.CostEstimate(flops=9 * 10**9, bytes_accessed=20 * 2**20, transcendentals=2**21),
    )(
        fields.reshape(ROWS, PLANE),
        cotangent.reshape(ROWS, PLANE),
        spectral_weight,
        jnp.asarray(plane),
        jnp.asarray(twiddle),
        jnp.asarray(spread),
        jnp.asarray(gather),
    )
    return grad_fields.reshape(1, XD, C, PLANE), grad_weight


def solution(mesh):
    placed = (
        P("dp", "pencil", None, None),
        P("dp", "pencil", None, None),
        P(None, None, "pencil", None),
    )
    return jax.shard_map(
        per_device,
        mesh=mesh,
        in_specs=placed,
        out_specs=(P("dp", "pencil", None, None), P("dp", None, "pencil", None)),
        check_vma=False,
    )
```

profile of v0, /device:TPU:1, one launch (start us, length us, event | category | flops | bytes accessed | tf_op | source)
XLA Modules:
  0.0 98.8 jit_solution(14813556501463920533)
XLA Ops:
  0.6 94.2 %shard_map.86 = (bf16[256,4096]{1,0:T(8,128)(2,1)}, f32[4,2,16,1024]{3,2,1,0:T(8,128)}) custom-call(bf16[256,4096]{1,0:T(8,128)(2,1)} %bitcast.4, bf16[256,4096]{1,0:T(8,128)(2,1)} %bitcast.5, bf16[32,2,16,1024]{3,2,1,0:T(8,128)(2,1)} %w_hbm.1, bf16[1024,4096]{1,0:T(8,128)(2,1)} %constant.8.clone.table_hbm, f32[32,2,256]{2,1,0:T(2,128)} %constant.9.clone.tw_ref, ...), custom_call_target="tpu_custom_call" | custom-call | flops 8999999488 | bytes 20971520 | tf_op jit(solution)/shard_map/pallas_call | solution.py:441
  94.8 0.0 copy-start
  94.8 3.2 %copy.11 = bf16[1,8,32,4096]{3,2,1,0:T(8,128)(2,1)} copy(bf16[1,8,32,4096]{3,2,1,0:T(8,128)(2,1)} %bitcast.3) | data formatting | bytes 4194304
  98.0 0.0 copy-done
  98.0 0.8 copy.12
Async XLA Ops:
  94.8 3.2 %copy-start = (f32[4,2,16,1024]{3,2,1,0:T(8,128)S(1)}, f32[4,2,16,1024]{3,2,1,0:T(8,128)}, u32[]{:S(2)}) copy-start(f32[4,2,16,1024]{3,2,1,0:T(8,128)} %get-tuple-element.9) | copy-start | bytes 1572868
where the time goes:
time: 98.9 us; the launch traced here: 98.8 us
  Pallas kernels  94.2 us (95%)
  local copies, waits for them, and re-layouts  3.98 us (4%)
    pallas_call x1, Pallas kernels, per_device(): pl.pallas_call(kernel, out_shape=(jax.ShapeDtypeStruct((ROWS, PLANE), BF1...  94.2 us
    unnamed x4, local copies, waits for them, and re-layouts  3.98 us

commit v1 on v0

v1 whole, which is shorter than its diff:
```python
import functools
import math

import jax
import jax.numpy as jnp
import numpy as np
from jax import lax
from jax.experimental import pallas as pl
from jax.experimental.pallas import tpu as pltpu
from jax.sharding import PartitionSpec as P

C = 32
MX = 32
MY = 32
MZ = 16
NX = 256
NY = 128
NZ = 32
PLANE = NY * NZ
PENCIL = 32
GROUPS = 8
XD = NX // PENCIL
ROWS = XD * C
SPEC = PENCIL * 2 * MZ
HALF = 128
FOLD = PLANE // 2
DEEP = MZ // 2
STACKS = 8
CORES = PENCIL // STACKS
MESH = pl.DeviceIdType.MESH
F32 = jnp.float32
BF16 = jnp.bfloat16

ROOT_HALF = 0.7071067811865476
DENSITY = 0.3989422804014327


def gelu_slope(v):
    return 0.5 * (1.0 + lax.erf(v * ROOT_HALF)) + v * jnp.exp(-0.5 * v * v) * DENSITY


@functools.lru_cache(None)
def tables():
    b = np.arange(MY)[None, :, None, None]
    c = 2 * np.arange(DEEP)[None, None, :, None] + np.arange(2)[:, None, None, None]
    p = np.arange(FOLD)[None, None, None, :]
    y, z = p % NY, p // NY
    turns = ((b - MY // 2) * y * NZ + c * z * NY) % PLANE
    angle = turns * (2.0 * math.pi / PLANE)
    plane = np.stack([np.cos(angle), -np.sin(angle)], axis=2).reshape(2, SPEC // 2, FOLD)
    kx = np.arange(MX)[:, None] - MX // 2
    j = np.arange(ROWS)[None, :] // C
    phase = ((kx * j) % NX) * (2.0 * math.pi / NX)
    twiddle = np.stack([np.cos(phase), np.sin(phase)], axis=1)
    lane = np.arange(HALF)
    pairs = np.arange(C * C)
    wide = (lane[:, None] % C) == (pairs[None, :] // C)
    again = (lane[:, None] % C) == (lane[None, :] % C)
    spread = np.tile(np.concatenate([wide, again], axis=1), (2, 1))
    first = wide * (lane[:, None] < C)
    gather = (pairs[:, None] // C) == (lane[None, :] % C)
    order = np.arange(HALF).reshape(4, 2, DEEP, 2).transpose(3, 0, 1, 2).reshape(-1)
    parity = np.zeros((HALF, HALF))
    parity[np.arange(HALF), order] = 1.0
    return (
        plane.astype(jnp.bfloat16),
        twiddle.astype(np.float32),
        spread.astype(jnp.bfloat16),
        first.astype(jnp.bfloat16),
        gather.astype(jnp.bfloat16),
        parity.astype(jnp.bfloat16),
    )


def times(value, angle, sign):
    re, im = value
    if angle == 0:
        return value
    co, si = math.cos(2 * math.pi * angle), sign * math.sin(2 * math.pi * angle)
    if angle in (0.125, 0.375):
        root = math.sqrt(0.5)
        if angle == 0.125:
            if sign > 0:
                return (re - im) * root, (re + im) * root
            return (re + im) * root, (im - re) * root
        if sign > 0:
            return (re + im) * (-root), (re - im) * root
        return (im - re) * root, (re + im) * (-root)
    return re * co - im * si, re * si + im * co


def add(a, b):
    return a[0] + b[0], a[1] + b[1]


def sub(a, b):
    return a[0] - b[0], a[1] - b[1]


def fft(values, sign):
    n = len(values)
    if n == 1:
        return values
    even, odd = fft(values[0::2], sign), fft(values[1::2], sign)
    out = [None] * n
    for k in range(n // 2):
        if k * 4 == n:
            re, im = odd[k]
            turned = (-im, re) if sign > 0 else (im, -re)
        else:
            turned = times(odd[k], k / n, sign)
        out[k] = add(even[k], turned)
        out[k + n // 2] = sub(even[k], turned)
    return out


def dot(a, b, dims):
    return lax.dot_general(a, b, (dims, ((), ())), preferred_element_type=F32)


def halves(value):
    high = value.astype(BF16)
    low = (value - high.astype(F32)).astype(BF16)
    return jnp.concatenate([high, low], axis=1)


def kernel(
    x_hbm, cot_hbm, w_hbm, table_hbm, tw_hbm, spread_hbm, first_hbm, gather_hbm, parity_hbm,
    out_hbm, gw_hbm,
    x_ref, cot_ref, w_ref, table, tw_ref, spread_ref, first_ref, gather_ref, parity_ref,
    send, recv, folded, even, weight, acc, spec, terms, mixed, dx, dg, out_ref, gw_ref,
    load_sem, own_sem, send_sem, recv_sem, dp_send, dp_recv, dp_own, store_sem,
):
    me = lax.axis_index("pencil")
    group = lax.axis_index("dp")
    stack, core = me // CORES, lax.rem(me, CORES)

    loads = [
        pltpu.make_async_copy(source, target, load_sem.at[place])
        for place, (source, target) in enumerate(
            [
                (x_hbm, x_ref),
                (table_hbm.at[0], table.at[0]),
                (table_hbm.at[1], table.at[1]),
                (parity_hbm, parity_ref),
                (w_hbm, w_ref),
                (tw_hbm, tw_ref),
                (spread_hbm, spread_ref),
                (gather_hbm, gather_ref),
                (first_hbm, first_ref),
                (cot_hbm, cot_ref),
            ]
        )
    ]
    for load in loads:
        load.start()

    barrier = pltpu.get_barrier_semaphore()

    def greet_pencil(i, carry):
        pl.semaphore_signal(
            barrier, inc=1, device_id=(group, lax.rem(me + i, PENCIL)), device_id_type=MESH
        )
        return carry

    def greet_group(i, carry):
        pl.semaphore_signal(
            barrier, inc=1, device_id=(lax.rem(group + i, GROUPS), me), device_id_type=MESH
        )
        return carry

    lax.fori_loop(1, PENCIL, greet_pencil, 0)
    lax.fori_loop(1, GROUPS, greet_group, 0)

    def block(ref, phase, parity, part, places):
        if part is None:
            return ref.at[phase, parity, places]
        return ref.at[phase, parity, places, part]

    def post(phase, parity, part, peer):
        slot = part or 0
        pltpu.make_async_remote_copy(
            src_ref=block(send, phase, parity, part, peer),
            dst_ref=block(recv, phase, parity, part, me),
            send_sem=send_sem.at[phase, parity, slot],
            recv_sem=recv_sem.at[phase, parity, slot],
            device_id=(group, peer),
            device_id_type=MESH,
        ).start()

    def own_copy(phase, parity, part):
        return pltpu.make_async_copy(
            block(send, phase, parity, part, me),
            block(recv, phase, parity, part, me),
            own_sem.at[phase, parity, part or 0],
        )

    def arrived(phase, parity, part):
        whole = block(recv, phase, parity, part, pl.ds(0, PENCIL - 1))
        pltpu.make_async_copy(whole, whole, recv_sem.at[phase, parity, part or 0]).wait()
        own_copy(phase, parity, part).wait()

    def sent(phase, parity, part):
        whole = block(send, phase, parity, part, pl.ds(0, PENCIL - 1))
        pltpu.make_async_copy(whole, whole, send_sem.at[phase, parity, part or 0]).wait()

    def stack_at(step):
        offset = STACKS // 2 + ((step + 1) // 2) * (2 * lax.rem(step, 2) - 1)
        return lax.rem(stack + offset + STACKS, STACKS)

    def post_stacks(phase, parity, part, steps):
        def one(i, carry):
            peer = stack_at(i // CORES) * CORES + lax.rem(core + i, CORES)

            @pl.when(peer != me)
            def _():
                post(phase, parity, part, peer)

            return carry

        lax.fori_loop(steps[0] * CORES, steps[1] * CORES, one, 0)

    def post_all(phase, parity, part):
        post_stacks(phase, parity, part, (0, STACKS))
        own_copy(phase, parity, part).start()

    lines_stack = CORES * 2 * DEEP

    def plane_forward(source, phase, parity, part, before_post=None):
        pieces = 2
        each = STACKS // pieces
        for piece in range(pieces):
            stacks = [stack_at(jnp.int32(piece * each + k)) for k in range(each)]
            lines = jnp.concatenate(
                [
                    table[parity, pl.ds(pl.multiple_of(at * lines_stack, lines_stack), lines_stack)]
                    for at in stacks
                ],
                axis=0,
            )
            result = dot(lines, source, ((1,), (1,))).astype(BF16)
            for k, at in enumerate(stacks):
                mine = result[k * lines_stack : (k + 1) * lines_stack]
                places = pl.ds(at * CORES, CORES)
                for place, half in enumerate((0, 1) if part is None else (part,)):
                    send[phase, parity, places, half] = mine[
                        :, place * HALF : (place + 1) * HALF
                    ].reshape(CORES, 2 * DEEP, HALF)
            if before_post is not None and piece == 0:
                before_post()
            post_stacks(phase, parity, part, (piece * each, (piece + 1) * each))
        own_copy(phase, parity, part).start()

    def first_forward(phase, parity, half):
        values = []
        for d in range(PENCIL):
            both = recv[phase, parity, d, half].astype(F32)
            values.append((both[:DEEP], both[DEEP:]))
        spectrum = fft(values, -1)
        for a in range(MX):
            re, im = spectrum[(a - MX // 2) % MX]
            co = tw_ref[a, 0:1, half * HALF : (half + 1) * HALF]
            si = tw_ref[a, 1:2, half * HALF : (half + 1) * HALF]
            for r, value in enumerate((re * co + im * si, im * co - re * si)):
                rows = slice(r * DEEP, (r + 1) * DEEP)
                acc[parity, a, rows] = value if half == 0 else acc[parity, a, rows] + value

    def first_inverse(phase, parity, half, scale):
        values = [None] * MX
        for a in range(MX):
            re, im = mixed[a, :DEEP], mixed[a, DEEP:]
            co = tw_ref[a, 0:1, half * HALF : (half + 1) * HALF]
            si = tw_ref[a, 1:2, half * HALF : (half + 1) * HALF]
            values[(a - MX // 2) % MX] = (re * co - im * si, im * co + re * si)
        signal = fft(values, 1)
        for d in range(PENCIL):
            both = jnp.concatenate(signal[d], axis=0)
            if scale is not None:
                both = both * scale
            send[phase, parity, d, half] = both.astype(BF16)

    def share_own(source, target, which):
        return pltpu.make_async_copy(
            source.at[pl.ds(group * (MX // GROUPS), MX // GROUPS)],
            target.at[group],
            dp_own.at[which],
        )

    def share(source, target, which):
        def one(i, carry):
            peer = lax.rem(group + i, GROUPS)
            pltpu.make_async_remote_copy(
                src_ref=source.at[pl.ds(peer * (MX // GROUPS), MX // GROUPS)],
                dst_ref=target.at[group],
                send_sem=dp_send.at[which],
                recv_sem=dp_recv.at[which],
                device_id=(peer, me),
                device_id_type=MESH,
            ).start()
            return carry

        lax.fori_loop(1, GROUPS, one, 0)
        share_own(source, target, which).start()

    def shared(source, target, which):
        whole = target.at[pl.ds(0, GROUPS - 1)]
        pltpu.make_async_copy(whole, whole, dp_recv.at[which]).wait()
        pltpu.make_async_copy(whole, whole, dp_send.at[which]).wait()
        share_own(source, target, which).wait()

    depth = lax.rem(lax.broadcasted_iota(jnp.int32, (2 * DEEP, HALF), 0), DEEP)
    volume = 1.0 / (NX * NY * NZ)
    scales = (
        jnp.where(depth == 0, volume, 2.0 * volume).astype(F32),
        jnp.full((2 * DEEP, HALF), 2.0 * volume, F32),
    )
    block_a = 8
    block_rows = block_a * 2 * DEEP
    lane_tiles = [slice(t * HALF, (t + 1) * HALF) for t in range(C * C // HALF)]

    def forward_mix(parity):
        def one(step, carry):
            own_a = pl.ds(step * block_a, block_a)
            lines = halves(acc[parity, own_a].reshape(block_rows, HALF))
            wide = dot(lines, spread_ref[...], ((1,), (0,)))
            spec[own_a, parity] = (
                wide[:, C * C :].astype(BF16).reshape(block_a, 2 * DEEP, HALF)
            )
            totals = []
            for a in range(block_a):
                out_re = jnp.zeros((DEEP, HALF), F32)
                out_im = jnp.zeros((DEEP, HALF), F32)
                row = a * 2 * DEEP
                for lanes in lane_tiles:
                    w_re = weight[parity, step * block_a + a, :DEEP, lanes]
                    w_im = weight[parity, step * block_a + a, DEEP:, lanes]
                    x_re = wide[row : row + DEEP, lanes]
                    x_im = wide[row + DEEP : row + 2 * DEEP, lanes]
                    out_re = out_re + x_re * w_re - x_im * w_im
                    out_im = out_im + x_re * w_im + x_im * w_re
                totals += [out_re, out_im]
            sums = dot(halves(jnp.concatenate(totals, axis=0)), spread_ref[:, C * C :], ((1,), (0,)))
            mixed[own_a] = sums.reshape(block_a, 2 * DEEP, HALF)
            return carry

        lax.fori_loop(0, MX // block_a, one, 0)

    def backward_mix(parity):
        def one(step, carry):
            own_a = pl.ds(step * block_a, block_a)
            lines = halves(acc[parity, own_a].reshape(block_rows, HALF))
            sums = dot(lines, spread_ref[:, C * C :], ((1,), (0,)))
            narrow = (sums.reshape(block_a, 2 * DEEP, HALF) * scales[parity]).astype(BF16)
            terms[own_a, parity] = narrow
            grads = narrow.astype(F32)
            products = []
            for a in range(block_a):
                g_re, g_im = grads[a, :DEEP], grads[a, DEEP:]
                tiles = []
                for lanes in lane_tiles:
                    w_re = weight[parity, step * block_a + a, :DEEP, lanes]
                    w_im = weight[parity, step * block_a + a, DEEP:, lanes]
                    tiles.append(
                        jnp.concatenate(
                            [g_re * w_re + g_im * w_im, g_im * w_re - g_re * w_im], axis=0
                        ).astype(BF16)
                    )
                products.append(jnp.concatenate(tiles, axis=1))
            result = dot(jnp.concatenate(products, axis=0), gather_ref[...], ((1,), (0,)))
            mixed[own_a] = result.reshape(block_a, 2 * DEEP, HALF)
            return carry

        lax.fori_loop(0, MX // block_a, one, 0)

    width = 512

    def lines_of(phase, parity, half):
        return recv[phase, parity, :, half].reshape(SPEC // 2, HALF)

    def even_cells(phase):
        lines = jnp.concatenate([lines_of(phase, 0, 0), lines_of(phase, 0, 1)], axis=1).T

        def one(step, carry):
            lanes = pl.ds(pl.multiple_of(step * width, width), width)
            even[:, lanes] = dot(lines, table[0, :, lanes], ((1,), (0,)))
            return carry

        lax.fori_loop(0, FOLD // width, one, 0)

    def odd_cells(phase, half, finish):
        lines = lines_of(phase, 1, half).T
        rows = pl.ds(half * HALF, HALF)

        def one(step, carry):
            near = pl.ds(pl.multiple_of(step * width, width), width)
            far = pl.ds(pl.multiple_of(FOLD + step * width, width), width)
            odd = dot(lines, table[1, :, near], ((1,), (0,)))
            base = even[rows, near]
            finish(rows, near, far, base + odd, base - odd)
            return carry

        lax.fori_loop(0, FOLD // width, one, 0)

    loads[0].wait()

    def fold_fields(step, carry):
        near = pl.ds(pl.multiple_of(step * width, width), width)
        far = pl.ds(pl.multiple_of(FOLD + step * width, width), width)
        one, two = x_ref[:, near].astype(F32), x_ref[:, far].astype(F32)
        folded[0, :, near] = (one + two).astype(BF16)
        folded[1, :, near] = (one - two).astype(BF16)
        return carry

    lax.fori_loop(0, FOLD // width, fold_fields, 0)
    loads[1].wait()

    def all_here():
        pl.semaphore_wait(barrier, PENCIL + GROUPS - 2)

    plane_forward(folded[0], 0, 0, None, all_here)
    loads[2].wait()
    plane_forward(folded[1], 0, 1, None)

    loads[3].wait()
    loads[4].wait()

    def part_weights(step, carry):
        own_a = pl.ds(step * 4, 4)
        lines = w_ref[own_a].reshape(HALF, C * C)
        apart = dot(parity_ref[...], lines, ((1,), (0,)))
        for parity in range(2):
            weight[parity, own_a] = apart[parity * HALF // 2 : (parity + 1) * HALF // 2].reshape(
                4, 2 * DEEP, C * C
            )
        return carry

    lax.fori_loop(0, MX // 4, part_weights, 0)
    for load in loads[5:]:
        load.wait()

    for parity in range(2):
        arrived(0, parity, None)
        for half in range(2):
            first_forward(0, parity, half)
        forward_mix(parity)
        for half in range(2):
            first_inverse(1, parity, half, scales[parity])
            if parity == 1:
                post_all(1, parity, half)
        if parity == 0:
            post_all(1, parity, None)
    share(spec, dx, 0)

    arrived(1, 0, None)
    even_cells(1)

    def slopes(rows, near, far, one, two):
        one = gelu_slope(one) * cot_ref[rows, near].astype(F32)
        two = gelu_slope(two) * cot_ref[rows, far].astype(F32)
        folded[0, rows, near] = (one + two).astype(BF16)
        folded[1, rows, near] = (one - two).astype(BF16)

    for half in range(2):
        arrived(1, 1, half)
        odd_cells(1, half, slopes)
        for parity in range(2):
            plane_forward(folded[parity, pl.ds(half * HALF, HALF)], 2, parity, half)

    for parity in range(2):
        arrived(2, parity, 0)
        first_forward(2, parity, 0)
    for parity in range(2):
        arrived(2, parity, 1)
        first_forward(2, parity, 1)
        backward_mix(parity)
        for half in range(2):
            first_inverse(3, parity, half, None)
            if parity == 1:
                post_all(3, parity, half)
        if parity == 0:
            post_all(3, parity, None)
    share(terms, dg, 1)

    shared(spec, dx, 0)
    shared(terms, dg, 1)

    def outer(a, carry):
        for parity in range(2):
            lines = jnp.concatenate([dx[s, a, parity] for s in range(GROUPS)], axis=0)
            wide = dot(lines, first_ref[...], ((1,), (0,)))
            factors = [dg[s, a, parity].astype(F32) for s in range(GROUPS)]
            for tile, lanes in enumerate(lane_tiles):
                out_re = jnp.zeros((DEEP, HALF), F32)
                out_im = jnp.zeros((DEEP, HALF), F32)
                for s in range(GROUPS):
                    row = s * 2 * DEEP
                    x_re, x_im = wide[row : row + DEEP, lanes], wide[row + DEEP : row + 2 * DEEP, lanes]
                    g_re, g_im = factors[s][:DEEP], factors[s][DEEP:]
                    out_re = out_re + x_re * g_re + x_im * g_im
                    out_im = out_im + x_re * g_im - x_im * g_re
                gw_ref[tile, a, 0, pl.ds(parity, DEEP, stride=2)] = out_re
                gw_ref[tile, a, 1, pl.ds(parity, DEEP, stride=2)] = out_im
        return carry

    lax.fori_loop(0, MX // GROUPS, outer, 0)
    stores = [
        pltpu.make_async_copy(gw_ref.at[tile], gw_hbm.at[:, :, :, lanes], store_sem.at[2 + tile])
        for tile, lanes in enumerate(lane_tiles)
    ]
    for store in stores:
        store.start()

    arrived(3, 0, None)
    even_cells(3)

    def finish(rows, near, far, one, two):
        out_ref[rows, near] = one.astype(BF16)
        out_ref[rows, far] = two.astype(BF16)

    for half in range(2):
        rows = pl.ds(half * HALF, HALF)
        arrived(3, 1, half)
        odd_cells(3, half, finish)
        pltpu.make_async_copy(out_ref.at[rows], out_hbm.at[rows], store_sem.at[half]).start()

    for parity in range(2):
        sent(0, parity, None)
        for half in range(2):
            sent(2, parity, half)
    for phase in (1, 3):
        sent(phase, 0, None)
        for half in range(2):
            sent(phase, 1, half)
    for half in range(2):
        rows = pl.ds(half * HALF, HALF)
        pltpu.make_async_copy(out_ref.at[rows], out_hbm.at[rows], store_sem.at[half]).wait()
    for store in stores:
        store.wait()


def per_device(fields, cotangent, spectral_weight):
    any_space = pl.BlockSpec(memory_space=pl.ANY)
    messages = (4, 2, PENCIL, 2, 2 * DEEP, HALF)
    spectrum = (MX, 2, 2 * DEEP, HALF)
    mine = MX // GROUPS
    constants = [jnp.asarray(table) for table in tables()]
    grad_fields, grad_weight = pl.pallas_call(
        kernel,
        out_shape=(
            jax.ShapeDtypeStruct((ROWS, PLANE), BF16),
            jax.ShapeDtypeStruct((mine, 2, MZ, C * C), F32),
        ),
        in_specs=[any_space] * (3 + len(constants)),
        out_specs=(any_space, any_space),
        scratch_shapes=[
            pltpu.VMEM((ROWS, PLANE), BF16),
            pltpu.VMEM((ROWS, PLANE), BF16),
            pltpu.VMEM((MX, 2, MZ, C * C), BF16),
        ]
        + [pltpu.VMEM(table.shape, table.dtype) for table in constants]
        + [
            pltpu.VMEM(messages, BF16),
            pltpu.VMEM(messages, BF16),
            pltpu.VMEM((2, ROWS, FOLD), BF16),
            pltpu.VMEM((ROWS, FOLD), F32),
            pltpu.VMEM((2, MX, 2 * DEEP, C * C), F32),
            pltpu.VMEM((2, MX, 2 * DEEP, HALF), F32),
            pltpu.VMEM(spectrum, BF16),
            pltpu.VMEM(spectrum, BF16),
            pltpu.VMEM((MX, 2 * DEEP, HALF), F32),
            pltpu.VMEM((GROUPS, mine, 2, 2 * DEEP, HALF), BF16),
            pltpu.VMEM((GROUPS, mine, 2, 2 * DEEP, HALF), BF16),
            pltpu.VMEM((ROWS, PLANE), BF16),
            pltpu.VMEM((C * C // HALF, mine, 2, MZ, HALF), F32),
            pltpu.SemaphoreType.DMA((10,)),
            pltpu.SemaphoreType.DMA((4, 2, 2)),
            pltpu.SemaphoreType.DMA((4, 2, 2)),
            pltpu.SemaphoreType.DMA((4, 2, 2)),
            pltpu.SemaphoreType.DMA((2,)),
            pltpu.SemaphoreType.DMA((2,)),
            pltpu.SemaphoreType.DMA((2,)),
            pltpu.SemaphoreType.DMA((2 + C * C // HALF,)),
        ],
        compiler_params=pltpu.CompilerParams(
            collective_id=0, has_side_effects=True, vmem_limit_bytes=60 * 2**20
        ),
        cost_estimate=pl.CostEstimate(
            flops=5 * 10**9, bytes_accessed=16 * 2**20, transcendentals=2**21
        ),
    )(
        fields.reshape(ROWS, PLANE),
        cotangent.reshape(ROWS, PLANE),
        spectral_weight,
        *constants,
    )
    return grad_fields.reshape(1, XD, C, PLANE), grad_weight


def solution(mesh):
    placed = (
        P("dp", "pencil", None, None),
        P("dp", "pencil", None, None),
        P(None, None, "pencil", None),
    )
    return jax.shard_map(
        per_device,
        mesh=mesh,
        in_specs=placed,
        out_specs=(P("dp", "pencil", None, None), P("dp", None, "pencil", None)),
        check_vma=False,
    )
```

time: 98.9 us -> 76 us (0.77)
  Pallas kernels: 94.2 us -> 70.6 us
    pallas_call x1, Pallas kernels: 94.2 us -> 70.6 us  [per_device(): pl.pallas_call(kernel, out_shape=(jax.ShapeDtypeStruct((ROWS, PLANE), BF1...]
where the time goes in v1:
time: 76 us; the launch traced here: 75.2 us
  Pallas kernels  70.6 us (93%)
  local copies, waits for them, and re-layouts  3.98 us (5%)
    pallas_call x1, Pallas kernels, per_device(): pl.pallas_call(kernel, out_shape=(jax.ShapeDtypeStruct((ROWS, PLANE), BF1...  70.6 us
    unnamed x4, local copies, waits for them, and re-layouts  3.98 us

profile of v1, /device:TPU:1, one launch (start us, length us, event | category | flops | bytes accessed | tf_op | source)
XLA Modules:
  0.0 75.2 jit_solution(18126654834803921798)
XLA Ops:
  0.6 70.6 %shard_map.104 = (bf16[256,4096]{1,0:T(8,128)(2,1)}, f32[4,2,16,1024]{3,2,1,0:T(8,128)}) custom-call(bf16[256,4096]{1,0:T(8,128)(2,1)} %bitcast.4, bf16[256,4096]{1,0:T(8,128)(2,1)} %bitcast.5, bf16[32,2,16,1024]{3,2,1,0:T(8,128)(2,1)} %w_hbm.1, bf16[2,512,2048]{2,1,0:T(8,128)(2,1)} %constant.12.clone.table_hbm, f32[32,2,256]{2,1,0:T(2,128)} %constant.13.clone.tw_hbm, ...), custom_call_target="tpu_custom_call" | custom-call | flops 5000000000 | bytes 16777216 | tf_op jit(solution)/shard_map/pallas_call | solution.py:547
  71.2 0.0 copy-start
  71.2 3.2 %copy.13 = bf16[1,8,32,4096]{3,2,1,0:T(8,128)(2,1)} copy(bf16[1,8,32,4096]{3,2,1,0:T(8,128)(2,1)} %bitcast.3) | data formatting | bytes 4194304
  74.4 0.0 copy-done
  74.4 0.8 %copy.14 = f32[4,2,16,1024]{3,2,1,0:T(8,128)} copy(f32[4,2,16,1024]{3,2,1,0:T(8,128)S(1)} %copy-done) | data formatting | bytes 1048576
Async XLA Ops:
  71.2 3.2 %copy-start = (f32[4,2,16,1024]{3,2,1,0:T(8,128)S(1)}, f32[4,2,16,1024]{3,2,1,0:T(8,128)}, u32[]{:S(2)}) copy-start(f32[4,2,16,1024]{3,2,1,0:T(8,128)} %get-tuple-element.9) | copy-start | bytes 1572868

commit v2 on v1

--- a/solution.py
+++ b/solution.py
@@ -25,6 +25,7 @@
 HALF = 128
 FOLD = PLANE // 2
 DEEP = MZ // 2
+STORES = 16
 STACKS = 8
 CORES = PENCIL // STACKS
 MESH = pl.DeviceIdType.MESH
@@ -126,10 +127,10 @@
 
 def kernel(
     x_hbm, cot_hbm, w_hbm, table_hbm, tw_hbm, spread_hbm, first_hbm, gather_hbm, parity_hbm,
-    out_hbm, gw_hbm,
+    out_ref, gw_ref,
     x_ref, cot_ref, w_ref, table, tw_ref, spread_ref, first_ref, gather_ref, parity_ref,
-    send, recv, folded, even, weight, acc, spec, terms, mixed, dx, dg, out_ref, gw_ref,
-    load_sem, own_sem, send_sem, recv_sem, dp_send, dp_recv, dp_own, store_sem,
+    send, recv, folded, even, weight, acc, spec, terms, mixed, dx, dg,
+    load_sem, own_sem, send_sem, recv_sem, dp_send, dp_recv, dp_own,
 ):
     me = lax.axis_index("pencil")
     group = lax.axis_index("dp")
@@ -152,7 +153,7 @@
             ]
         )
     ]
-    for load in loads:
+    for load in loads[:2]:
         load.start()
 
     barrier = pltpu.get_barrier_semaphore()
@@ -279,34 +280,36 @@
                 both = both * scale
             send[phase, parity, d, half] = both.astype(BF16)
 
-    def share_own(source, target, which):
+    mine_a = MX // GROUPS
+
+    def share_own(source, target, which, parity):
         return pltpu.make_async_copy(
-            source.at[pl.ds(group * (MX // GROUPS), MX // GROUPS)],
-            target.at[group],
-            dp_own.at[which],
+            source.at[parity, pl.ds(group * mine_a, mine_a)],
+            target.at[parity, group],
+            dp_own.at[which, parity],
         )
 
-    def share(source, target, which):
+    def share(source, target, which, parity):
         def one(i, carry):
             peer = lax.rem(group + i, GROUPS)
             pltpu.make_async_remote_copy(
-                src_ref=source.at[pl.ds(peer * (MX // GROUPS), MX // GROUPS)],
-                dst_ref=target.at[group],
-                send_sem=dp_send.at[which],
-                recv_sem=dp_recv.at[which],
+                src_ref=source.at[parity, pl.ds(peer * mine_a, mine_a)],
+                dst_ref=target.at[parity, group],
+                send_sem=dp_send.at[which, parity],
+                recv_sem=dp_recv.at[which, parity],
                 device_id=(peer, me),
                 device_id_type=MESH,
             ).start()
             return carry
 
         lax.fori_loop(1, GROUPS, one, 0)
-        share_own(source, target, which).start()
-
-    def shared(source, target, which):
-        whole = target.at[pl.ds(0, GROUPS - 1)]
-        pltpu.make_async_copy(whole, whole, dp_recv.at[which]).wait()
-        pltpu.make_async_copy(whole, whole, dp_send.at[which]).wait()
-        share_own(source, target, which).wait()
+        share_own(source, target, which, parity).start()
+
+    def shared(source, target, which, parity):
+        whole = target.at[parity, pl.ds(0, GROUPS - 1)]
+        pltpu.make_async_copy(whole, whole, dp_recv.at[which, parity]).wait()
+        pltpu.make_async_copy(whole, whole, dp_send.at[which, parity]).wait()
+        share_own(source, target, which, parity).wait()
 
     depth = lax.rem(lax.broadcasted_iota(jnp.int32, (2 * DEEP, HALF), 0), DEEP)
     volume = 1.0 / (NX * NY * NZ)
@@ -323,7 +326,7 @@
             own_a = pl.ds(step * block_a, block_a)
             lines = halves(acc[parity, own_a].reshape(block_rows, HALF))
             wide = dot(lines, spread_ref[...], ((1,), (0,)))
-            spec[own_a, parity] = (
+            spec[parity, own_a] = (
                 wide[:, C * C :].astype(BF16).reshape(block_a, 2 * DEEP, HALF)
             )
             totals = []
@@ -351,7 +354,7 @@
             lines = halves(acc[parity, own_a].reshape(block_rows, HALF))
             sums = dot(lines, spread_ref[:, C * C :], ((1,), (0,)))
             narrow = (sums.reshape(block_a, 2 * DEEP, HALF) * scales[parity]).astype(BF16)
-            terms[own_a, parity] = narrow
+            terms[parity, own_a] = narrow
             grads = narrow.astype(F32)
             products = []
             for a in range(block_a):
@@ -399,16 +402,18 @@
             finish(rows, near, far, base + odd, base - odd)
             return carry
 
-        lax.fori_loop(0, FOLD // width, one, 0)
+        lax.fori_loop(0, FOLD // width, one, 0, unroll=True)
 
     loads[0].wait()
+    for load in loads[2:]:
+        load.start()
 
     def fold_fields(step, carry):
         near = pl.ds(pl.multiple_of(step * width, width), width)
         far = pl.ds(pl.multiple_of(FOLD + step * width, width), width)
-        one, two = x_ref[:, near].astype(F32), x_ref[:, far].astype(F32)
-        folded[0, :, near] = (one + two).astype(BF16)
-        folded[1, :, near] = (one - two).astype(BF16)
+        one, two = x_ref[:, near], x_ref[:, far]
+        folded[0, :, near] = one + two
+        folded[1, :, near] = one - two
         return carry
 
     lax.fori_loop(0, FOLD // width, fold_fields, 0)
@@ -443,13 +448,13 @@
         for half in range(2):
             first_forward(0, parity, half)
         forward_mix(parity)
+        share(spec, dx, 0, parity)
         for half in range(2):
             first_inverse(1, parity, half, scales[parity])
             if parity == 1:
                 post_all(1, parity, half)
         if parity == 0:
             post_all(1, parity, None)
-    share(spec, dx, 0)
 
     arrived(1, 0, None)
     even_cells(1)
@@ -473,22 +478,23 @@
         arrived(2, parity, 1)
         first_forward(2, parity, 1)
         backward_mix(parity)
+        share(terms, dg, 1, parity)
         for half in range(2):
             first_inverse(3, parity, half, None)
             if parity == 1:
                 post_all(3, parity, half)
         if parity == 0:
             post_all(3, parity, None)
-    share(terms, dg, 1)
-
-    shared(spec, dx, 0)
-    shared(terms, dg, 1)
+
+    for parity in range(2):
+        shared(spec, dx, 0, parity)
+        shared(terms, dg, 1, parity)
 
     def outer(a, carry):
         for parity in range(2):
-            lines = jnp.concatenate([dx[s, a, parity] for s in range(GROUPS)], axis=0)
+            lines = dx[parity, :, a].reshape(HALF, HALF)
             wide = dot(lines, first_ref[...], ((1,), (0,)))
-            factors = [dg[s, a, parity].astype(F32) for s in range(GROUPS)]
+            factors = [dg[parity, s, a].astype(F32) for s in range(GROUPS)]
             for tile, lanes in enumerate(lane_tiles):
                 out_re = jnp.zeros((DEEP, HALF), F32)
                 out_im = jnp.zeros((DEEP, HALF), F32)
@@ -503,13 +509,6 @@
         return carry
 
     lax.fori_loop(0, MX // GROUPS, outer, 0)
-    stores = [
-        pltpu.make_async_copy(gw_ref.at[tile], gw_hbm.at[:, :, :, lanes], store_sem.at[2 + tile])
-        for tile, lanes in enumerate(lane_tiles)
-    ]
-    for store in stores:
-        store.start()
-
     arrived(3, 0, None)
     even_cells(3)
 
@@ -518,10 +517,8 @@
         out_ref[rows, far] = two.astype(BF16)
 
     for half in range(2):
-        rows = pl.ds(half * HALF, HALF)
         arrived(3, 1, half)
         odd_cells(3, half, finish)
-        pltpu.make_async_copy(out_ref.at[rows], out_hbm.at[rows], store_sem.at[half]).start()
 
     for parity in range(2):
         sent(0, parity, None)
@@ -531,27 +528,41 @@
         sent(phase, 0, None)
         for half in range(2):
             sent(phase, 1, half)
-    for half in range(2):
-        rows = pl.ds(half * HALF, HALF)
-        pltpu.make_async_copy(out_ref.at[rows], out_hbm.at[rows], store_sem.at[half]).wait()
-    for store in stores:
-        store.wait()
+
+
+def store_kernel(out_ref, gw_ref, out_hbm, gw_hbm, sems):
+    copies = []
+    for place in range(STORES):
+        rows = pl.ds(place * (ROWS // STORES), ROWS // STORES)
+        copies.append(pltpu.make_async_copy(out_ref.at[rows], out_hbm.at[rows], sems.at[place]))
+    for tile in range(C * C // HALF):
+        lanes = slice(tile * HALF, (tile + 1) * HALF)
+        copies.append(
+            pltpu.make_async_copy(
+                gw_ref.at[tile], gw_hbm.at[:, :, :, lanes], sems.at[STORES + tile]
+            )
+        )
+    for copy in copies:
+        copy.start()
+    for copy in copies:
+        copy.wait()
 
 
 def per_device(fields, cotangent, spectral_weight):
     any_space = pl.BlockSpec(memory_space=pl.ANY)
+    vmem = pl.BlockSpec(memory_space=pltpu.VMEM)
     messages = (4, 2, PENCIL, 2, 2 * DEEP, HALF)
-    spectrum = (MX, 2, 2 * DEEP, HALF)
+    spectrum = (2, MX, 2 * DEEP, HALF)
     mine = MX // GROUPS
     constants = [jnp.asarray(table) for table in tables()]
     grad_fields, grad_weight = pl.pallas_call(
         kernel,
         out_shape=(
-            jax.ShapeDtypeStruct((ROWS, PLANE), BF16),
-            jax.ShapeDtypeStruct((mine, 2, MZ, C * C), F32),
+            pltpu.VMEM((ROWS, PLANE), BF16),
+            pltpu.VMEM((C * C // HALF, mine, 2, MZ, HALF), F32),
         ),
         in_specs=[any_space] * (3 + len(constants)),
-        out_specs=(any_space, any_space),
+        out_specs=(vmem, vmem),
         scratch_shapes=[
             pltpu.VMEM((ROWS, PLANE), BF16),
             pltpu.VMEM((ROWS, PLANE), BF16),
@@ -568,30 +579,46 @@
             pltpu.VMEM(spectrum, BF16),
             pltpu.VMEM(spectrum, BF16),
             pltpu.VMEM((MX, 2 * DEEP, HALF), F32),
-            pltpu.VMEM((GROUPS, mine, 2, 2 * DEEP, HALF), BF16),
-            pltpu.VMEM((GROUPS, mine, 2, 2 * DEEP, HALF), BF16),
-            pltpu.VMEM((ROWS, PLANE), BF16),
-            pltpu.VMEM((C * C // HALF, mine, 2, MZ, HALF), F32),
+            pltpu.VMEM((2, GROUPS, mine, 2 * DEEP, HALF), BF16),
+            pltpu.VMEM((2, GROUPS, mine, 2 * DEEP, HALF), BF16),
             pltpu.SemaphoreType.DMA((10,)),
             pltpu.SemaphoreType.DMA((4, 2, 2)),
             pltpu.SemaphoreType.DMA((4, 2, 2)),
             pltpu.SemaphoreType.DMA((4, 2, 2)),
-            pltpu.SemaphoreType.DMA((2,)),
-            pltpu.SemaphoreType.DMA((2,)),
-            pltpu.SemaphoreType.DMA((2,)),
-            pltpu.SemaphoreType.DMA((2 + C * C // HALF,)),
+            pltpu.SemaphoreType.DMA((2, 2)),
+            pltpu.SemaphoreType.DMA((2, 2)),
+            pltpu.SemaphoreType.DMA((2, 2)),
         ],
         compiler_params=pltpu.CompilerParams(
-            collective_id=0, has_side_effects=True, vmem_limit_bytes=60 * 2**20
+            collective_id=0, has_side_effects=True, vmem_limit_bytes=56 * 2**20
         ),
         cost_estimate=pl.CostEstimate(
             flops=5 * 10**9, bytes_accessed=16 * 2**20, transcendentals=2**21
         ),
     )(
-        fields.reshape(ROWS, PLANE),
-        cotangent.reshape(ROWS, PLANE),
-        spectral_weight,
-        *constants,
+        *(
+            pltpu.with_memory_space_constraint(operand, pltpu.HBM)
+            for operand in (
+                fields.reshape(ROWS, PLANE),
+                cotangent.reshape(ROWS, PLANE),
+                spectral_weight,
+                *constants,
+            )
+        )
+    )
+    grad_fields, grad_weight = pl.pallas_call(
+        store_kernel,
+        out_shape=(
+            jax.ShapeDtypeStruct((ROWS, PLANE), BF16),
+            jax.ShapeDtypeStruct((mine, 2, MZ, C * C), F32),
+        ),
+        in_specs=[vmem, vmem],
+        out_specs=(any_space, any_space),
+        scratch_shapes=[pltpu.SemaphoreType.DMA((STORES + C * C // HALF,))],
+        compiler_params=pltpu.CompilerParams(vmem_limit_bytes=2 * 2**20),
+    )(
+        pltpu.with_memory_space_constraint(grad_fields, pltpu.VMEM),
+        pltpu.with_memory_space_constraint(grad_weight, pltpu.VMEM),
     )
     return grad_fields.reshape(1, XD, C, PLANE), grad_weight
 

time: 76 us -> 69.4 us (0.913)
  local copies, waits for them, and re-layouts: 3.98 us -> 0 us
  Pallas kernels: 70.6 us -> 68.6 us
    unnamed x4 -> x0, local copies, waits for them, and re-layouts: 3.98 us -> none
    pallas_call x1 -> x2, Pallas kernels: 70.6 us -> 68.6 us  [the longest x1 67 us: per_device(): pl.pallas_call(kernel, out_shape=(pltpu.VMEM((ROWS, PLANE), BF16), pltpu....]
where the time goes in v2:
time: 69.4 us; the launch traced here: 69.3 us
  Pallas kernels  68.6 us (99%)
    pallas_call x1, Pallas kernels, per_device(): pl.pallas_call(kernel, out_shape=(pltpu.VMEM((ROWS, PLANE), BF16), pltpu....  67 us
    pallas_call x1, Pallas kernels, per_device(): pl.pallas_call(store_kernel, out_shape=(jax.ShapeDtypeStruct((ROWS, PLANE...  1.68 us

profile of v2, /device:TPU:1, one launch (start us, length us, event | category | flops | bytes accessed | tf_op | source)
XLA Modules:
  0.0 69.3 jit_solution(15713714991310987102)
XLA Ops:
  0.6 67.0 %shard_map.104 = (bf16[256,4096]{1,0:T(8,128)(2,1)S(1)}, f32[8,4,2,16,128]{4,3,2,1,0:T(8,128)S(1)}) custom-call(bf16[256,4096]{1,0:T(8,128)(2,1)} %bitcast.3, bf16[256,4096]{1,0:T(8,128)(2,1)} %bitcast.4, bf16[32,2,16,1024]{3,2,1,0:T(8,128)(2,1)} %w_hbm.1, bf16[2,512,2048]{2,1,0:T(8,128)(2,1)} %constant.12.clone.table_hbm, ...), custom_call_target="tpu_custom_call" | custom-call | flops 5000000000 | bytes 16777216 | tf_op jit(solution)/shard_map/pallas_call | solution.py:558
  67.6 1.7 %shard_map.105 = (bf16[256,4096]{1,0:T(8,128)(2,1)}, f32[4,2,16,1024]{3,2,1,0:T(8,128)}) custom-call(bf16[256,4096]{1,0:T(8,128)(2,1)S(1)} %get-tuple-element.6.out_ref, f32[8,4,2,16,128]{4,3,2,1,0:T(8,128)S(1)} %get-tuple-element.7.gw_ref), custom_call_target="tpu_custom_call" | custom-call | tf_op jit(solution)/shard_map/pallas_call | solution.py:609

commit v3 on v2

--- a/solution.py
+++ b/solution.py
@@ -25,7 +25,7 @@
 HALF = 128
 FOLD = PLANE // 2
 DEEP = MZ // 2
-STORES = 16
+STORES = 8
 STACKS = 8
 CORES = PENCIL // STACKS
 MESH = pl.DeviceIdType.MESH
@@ -127,22 +127,45 @@
 
 def kernel(
     x_hbm, cot_hbm, w_hbm, table_hbm, tw_hbm, spread_hbm, first_hbm, gather_hbm, parity_hbm,
-    out_ref, gw_ref,
-    x_ref, cot_ref, w_ref, table, tw_ref, spread_ref, first_ref, gather_ref, parity_ref,
-    send, recv, folded, even, weight, acc, spec, terms, mixed, dx, dg,
-    load_sem, own_sem, send_sem, recv_sem, dp_send, dp_recv, dp_own,
+    out_ref, gw_ref, odd_table, even, tail_ref,
+    x_ref, cot_ref, w_ref, even_table, tw_ref, spread_ref, first_ref, gather_ref, parity_ref,
+    send, recv, folded, weight, acc, spec, terms, mixed, dx, dg,
+    x_sem, table_sem, load_sem, own_sem, send_sem, recv_sem, dp_send, dp_recv, dp_own,
 ):
+    table = (even_table, odd_table)
     me = lax.axis_index("pencil")
     group = lax.axis_index("dp")
     stack, core = me // CORES, lax.rem(me, CORES)
 
+    width = 512
+    blocks = FOLD // width
+    lines_stack = CORES * 2 * DEEP
+
+    def stack_at(step):
+        offset = STACKS // 2 + ((step + 1) // 2) * (2 * lax.rem(step, 2) - 1)
+        return lax.rem(stack + offset + STACKS, STACKS)
+
+    def stack_lines(step):
+        return pl.ds(pl.multiple_of(stack_at(jnp.int32(step)) * lines_stack, lines_stack), lines_stack)
+
+    load_x = []
+    for step in range(blocks):
+        for far in range(2):
+            lanes = pl.ds(far * FOLD + step * width, width)
+            load_x.append(
+                pltpu.make_async_copy(x_hbm.at[:, lanes], x_ref.at[:, lanes], x_sem.at[step, far])
+            )
+    load_table = [
+        pltpu.make_async_copy(
+            table_hbm.at[0, stack_lines(step)], even_table.at[stack_lines(step)], table_sem.at[step]
+        )
+        for step in range(STACKS)
+    ]
     loads = [
         pltpu.make_async_copy(source, target, load_sem.at[place])
         for place, (source, target) in enumerate(
             [
-                (x_hbm, x_ref),
-                (table_hbm.at[0], table.at[0]),
-                (table_hbm.at[1], table.at[1]),
+                (table_hbm.at[1], odd_table),
                 (parity_hbm, parity_ref),
                 (w_hbm, w_ref),
                 (tw_hbm, tw_ref),
@@ -153,7 +176,7 @@
             ]
         )
     ]
-    for load in loads[:2]:
+    for load in load_x + load_table:
         load.start()
 
     barrier = pltpu.get_barrier_semaphore()
@@ -205,10 +228,6 @@
         whole = block(send, phase, parity, part, pl.ds(0, PENCIL - 1))
         pltpu.make_async_copy(whole, whole, send_sem.at[phase, parity, part or 0]).wait()
 
-    def stack_at(step):
-        offset = STACKS // 2 + ((step + 1) // 2) * (2 * lax.rem(step, 2) - 1)
-        return lax.rem(stack + offset + STACKS, STACKS)
-
     def post_stacks(phase, parity, part, steps):
         def one(i, carry):
             peer = stack_at(i // CORES) * CORES + lax.rem(core + i, CORES)
@@ -225,24 +244,19 @@
         post_stacks(phase, parity, part, (0, STACKS))
         own_copy(phase, parity, part).start()
 
-    lines_stack = CORES * 2 * DEEP
-
-    def plane_forward(source, phase, parity, part, before_post=None):
+    def plane_forward(source, phase, parity, part, ready=None, before_post=None):
         pieces = 2
         each = STACKS // pieces
         for piece in range(pieces):
-            stacks = [stack_at(jnp.int32(piece * each + k)) for k in range(each)]
-            lines = jnp.concatenate(
-                [
-                    table[parity, pl.ds(pl.multiple_of(at * lines_stack, lines_stack), lines_stack)]
-                    for at in stacks
-                ],
-                axis=0,
-            )
+            steps = range(piece * each, (piece + 1) * each)
+            if ready is not None:
+                for step in steps:
+                    ready[step].wait()
+            lines = jnp.concatenate([table[parity][stack_lines(step)] for step in steps], axis=0)
             result = dot(lines, source, ((1,), (1,))).astype(BF16)
-            for k, at in enumerate(stacks):
+            for k, step in enumerate(steps):
                 mine = result[k * lines_stack : (k + 1) * lines_stack]
-                places = pl.ds(at * CORES, CORES)
+                places = pl.ds(stack_at(jnp.int32(step)) * CORES, CORES)
                 for place, half in enumerate((0, 1) if part is None else (part,)):
                     send[phase, parity, places, half] = mine[
                         :, place * HALF : (place + 1) * HALF
@@ -346,7 +360,7 @@
             mixed[own_a] = sums.reshape(block_a, 2 * DEEP, HALF)
             return carry
 
-        lax.fori_loop(0, MX // block_a, one, 0)
+        lax.fori_loop(0, MX // block_a, one, 0, unroll=2)
 
     def backward_mix(parity):
         def one(step, carry):
@@ -373,19 +387,22 @@
             mixed[own_a] = result.reshape(block_a, 2 * DEEP, HALF)
             return carry
 
-        lax.fori_loop(0, MX // block_a, one, 0)
-
-    width = 512
+        lax.fori_loop(0, MX // block_a, one, 0, unroll=2)
 
     def lines_of(phase, parity, half):
         return recv[phase, parity, :, half].reshape(SPEC // 2, HALF)
 
-    def even_cells(phase):
-        lines = jnp.concatenate([lines_of(phase, 0, 0), lines_of(phase, 0, 1)], axis=1).T
+    def even_cells(phase, half):
+        if half is None:
+            lines = jnp.concatenate([lines_of(phase, 0, 0), lines_of(phase, 0, 1)], axis=1).T
+            rows = pl.ds(0, ROWS)
+        else:
+            lines = lines_of(phase, 0, half).T
+            rows = pl.ds(half * HALF, HALF)
 
         def one(step, carry):
             lanes = pl.ds(pl.multiple_of(step * width, width), width)
-            even[:, lanes] = dot(lines, table[0, :, lanes], ((1,), (0,)))
+            even[rows, lanes] = dot(lines, even_table[:, lanes], ((1,), (0,)))
             return carry
 
         lax.fori_loop(0, FOLD // width, one, 0)
@@ -397,37 +414,32 @@
         def one(step, carry):
             near = pl.ds(pl.multiple_of(step * width, width), width)
             far = pl.ds(pl.multiple_of(FOLD + step * width, width), width)
-            odd = dot(lines, table[1, :, near], ((1,), (0,)))
+            odd = dot(lines, odd_table[:, near], ((1,), (0,)))
             base = even[rows, near]
             finish(rows, near, far, base + odd, base - odd)
             return carry
 
         lax.fori_loop(0, FOLD // width, one, 0, unroll=True)
 
-    loads[0].wait()
-    for load in loads[2:]:
-        load.start()
-
-    def fold_fields(step, carry):
-        near = pl.ds(pl.multiple_of(step * width, width), width)
-        far = pl.ds(pl.multiple_of(FOLD + step * width, width), width)
+    for step in range(blocks):
+        near, far = pl.ds(step * width, width), pl.ds(FOLD + step * width, width)
+        load_x[2 * step].wait()
+        load_x[2 * step + 1].wait()
         one, two = x_ref[:, near], x_ref[:, far]
         folded[0, :, near] = one + two
         folded[1, :, near] = one - two
-        return carry
-
-    lax.fori_loop(0, FOLD // width, fold_fields, 0)
-    loads[1].wait()
+    for load in loads:
+        load.start()
 
     def all_here():
         pl.semaphore_wait(barrier, PENCIL + GROUPS - 2)
 
-    plane_forward(folded[0], 0, 0, None, all_here)
+    plane_forward(folded[0], 0, 0, None, load_table, all_here)
+    loads[0].wait()
+    plane_forward(folded[1], 0, 1, None)
+
+    loads[1].wait()
     loads[2].wait()
-    plane_forward(folded[1], 0, 1, None)
-
-    loads[3].wait()
-    loads[4].wait()
 
     def part_weights(step, carry):
         own_a = pl.ds(step * 4, 4)
@@ -440,7 +452,7 @@
         return carry
 
     lax.fori_loop(0, MX // 4, part_weights, 0)
-    for load in loads[5:]:
+    for load in loads[3:]:
         load.wait()
 
     for parity in range(2):
@@ -448,16 +460,13 @@
         for half in range(2):
             first_forward(0, parity, half)
         forward_mix(parity)
-        share(spec, dx, 0, parity)
         for half in range(2):
             first_inverse(1, parity, half, scales[parity])
-            if parity == 1:
-                post_all(1, parity, half)
-        if parity == 0:
-            post_all(1, parity, None)
-
-    arrived(1, 0, None)
-    even_cells(1)
+            if half == 0:
+                post_all(1, parity, 0)
+    for parity in range(2):
+        post_all(1, parity, 1)
+
 
     def slopes(rows, near, far, one, two):
         one = gelu_slope(one) * cot_ref[rows, near].astype(F32)
@@ -466,10 +475,14 @@
         folded[1, rows, near] = (one - two).astype(BF16)
 
     for half in range(2):
+        arrived(1, 0, half)
+        even_cells(1, half)
         arrived(1, 1, half)
         odd_cells(1, half, slopes)
         for parity in range(2):
             plane_forward(folded[parity, pl.ds(half * HALF, HALF)], 2, parity, half)
+    for parity in range(2):
+        share(spec, dx, 0, parity)
 
     for parity in range(2):
         arrived(2, parity, 0)
@@ -508,44 +521,64 @@
                 gw_ref[tile, a, 1, pl.ds(parity, DEEP, stride=2)] = out_im
         return carry
 
-    lax.fori_loop(0, MX // GROUPS, outer, 0)
+    lax.fori_loop(0, MX // GROUPS, outer, 0, unroll=2)
     arrived(3, 0, None)
-    even_cells(3)
+    even_cells(3, None)
 
     def finish(rows, near, far, one, two):
         out_ref[rows, near] = one.astype(BF16)
         out_ref[rows, far] = two.astype(BF16)
 
-    for half in range(2):
-        arrived(3, 1, half)
-        odd_cells(3, half, finish)
+    arrived(3, 1, 0)
+    odd_cells(3, 0, finish)
+    arrived(3, 1, 1)
+    tail_ref[...] = lines_of(3, 1, 1).T
 
     for parity in range(2):
         sent(0, parity, None)
         for half in range(2):
             sent(2, parity, half)
-    for phase in (1, 3):
-        sent(phase, 0, None)
         for half in range(2):
-            sent(phase, 1, half)
-
-
-def store_kernel(out_ref, gw_ref, out_hbm, gw_hbm, sems):
-    copies = []
+            sent(1, parity, half)
+    sent(3, 0, None)
+    for half in range(2):
+        sent(3, 1, half)
+
+
+def last_kernel(
+    out_ref, gw_ref, table_ref, even_ref, lines_ref, out_hbm, gw_hbm, tail, store_sem, tail_sem
+):
+    stores = []
     for place in range(STORES):
-        rows = pl.ds(place * (ROWS // STORES), ROWS // STORES)
-        copies.append(pltpu.make_async_copy(out_ref.at[rows], out_hbm.at[rows], sems.at[place]))
+        rows = pl.ds(place * (HALF // STORES), HALF // STORES)
+        stores.append(
+            pltpu.make_async_copy(out_ref.at[rows], out_hbm.at[rows], store_sem.at[place])
+        )
     for tile in range(C * C // HALF):
         lanes = slice(tile * HALF, (tile + 1) * HALF)
-        copies.append(
+        stores.append(
             pltpu.make_async_copy(
-                gw_ref.at[tile], gw_hbm.at[:, :, :, lanes], sems.at[STORES + tile]
+                gw_ref.at[tile], gw_hbm.at[:, :, :, lanes], store_sem.at[STORES + tile]
             )
         )
-    for copy in copies:
-        copy.start()
-    for copy in copies:
-        copy.wait()
+    for store in stores:
+        store.start()
+    width = 512
+    rows = pl.ds(HALF, HALF)
+    for step in range(FOLD // width):
+        near, far = pl.ds(step * width, width), pl.ds(FOLD + step * width, width)
+        odd = dot(lines_ref[...], table_ref[:, near], ((1,), (0,)))
+        base = even_ref[rows, near]
+        tail[:, near] = (base + odd).astype(BF16)
+        tail[:, far] = (base - odd).astype(BF16)
+        for place, lanes in enumerate((near, far)):
+            store = pltpu.make_async_copy(
+                tail.at[:, lanes], out_hbm.at[rows, lanes], tail_sem.at[step, place]
+            )
+            store.start()
+            stores.append(store)
+    for store in stores:
+        store.wait()
 
 
 def per_device(fields, cotangent, spectral_weight):
@@ -555,25 +588,28 @@
     spectrum = (2, MX, 2 * DEEP, HALF)
     mine = MX // GROUPS
     constants = [jnp.asarray(table) for table in tables()]
-    grad_fields, grad_weight = pl.pallas_call(
+    results = pl.pallas_call(
         kernel,
         out_shape=(
-            pltpu.VMEM((ROWS, PLANE), BF16),
+            pltpu.VMEM((HALF, PLANE), BF16),
             pltpu.VMEM((C * C // HALF, mine, 2, MZ, HALF), F32),
+            pltpu.VMEM((SPEC // 2, FOLD), BF16),
+            pltpu.VMEM((ROWS, FOLD), F32),
+            pltpu.VMEM((HALF, SPEC // 2), BF16),
         ),
         in_specs=[any_space] * (3 + len(constants)),
-        out_specs=(vmem, vmem),
+        out_specs=(vmem,) * 5,
         scratch_shapes=[
             pltpu.VMEM((ROWS, PLANE), BF16),
             pltpu.VMEM((ROWS, PLANE), BF16),
             pltpu.VMEM((MX, 2, MZ, C * C), BF16),
         ]
-        + [pltpu.VMEM(table.shape, table.dtype) for table in constants]
+        + [pltpu.VMEM(constants[0].shape[1:], BF16)]
+        + [pltpu.VMEM(table.shape, table.dtype) for table in constants[1:]]
         + [
             pltpu.VMEM(messages, BF16),
             pltpu.VMEM(messages, BF16),
             pltpu.VMEM((2, ROWS, FOLD), BF16),
-            pltpu.VMEM((ROWS, FOLD), F32),
             pltpu.VMEM((2, MX, 2 * DEEP, C * C), F32),
             pltpu.VMEM((2, MX, 2 * DEEP, HALF), F32),
             pltpu.VMEM(spectrum, BF16),
@@ -581,7 +617,9 @@
             pltpu.VMEM((MX, 2 * DEEP, HALF), F32),
             pltpu.VMEM((2, GROUPS, mine, 2 * DEEP, HALF), BF16),
             pltpu.VMEM((2, GROUPS, mine, 2 * DEEP, HALF), BF16),
-            pltpu.SemaphoreType.DMA((10,)),
+            pltpu.SemaphoreType.DMA((4, 2)),
+            pltpu.SemaphoreType.DMA((STACKS,)),
+            pltpu.SemaphoreType.DMA((8,)),
             pltpu.SemaphoreType.DMA((4, 2, 2)),
             pltpu.SemaphoreType.DMA((4, 2, 2)),
             pltpu.SemaphoreType.DMA((4, 2, 2)),
@@ -590,7 +628,7 @@
             pltpu.SemaphoreType.DMA((2, 2)),
         ],
         compiler_params=pltpu.CompilerParams(
-            collective_id=0, has_side_effects=True, vmem_limit_bytes=56 * 2**20
+            collective_id=0, has_side_effects=True, vmem_limit_bytes=48 * 2**20
         ),
         cost_estimate=pl.CostEstimate(
             flops=5 * 10**9, bytes_accessed=16 * 2**20, transcendentals=2**21
@@ -607,19 +645,20 @@
         )
     )
     grad_fields, grad_weight = pl.pallas_call(
-        store_kernel,
+        last_kernel,
         out_shape=(
             jax.ShapeDtypeStruct((ROWS, PLANE), BF16),
             jax.ShapeDtypeStruct((mine, 2, MZ, C * C), F32),
         ),
-        in_specs=[vmem, vmem],
+        in_specs=[vmem] * 5,
         out_specs=(any_space, any_space),
-        scratch_shapes=[pltpu.SemaphoreType.DMA((STORES + C * C // HALF,))],
-        compiler_params=pltpu.CompilerParams(vmem_limit_bytes=2 * 2**20),
-    )(
-        pltpu.with_memory_space_constraint(grad_fields, pltpu.VMEM),
-        pltpu.with_memory_space_constraint(grad_weight, pltpu.VMEM),
-    )
+        scratch_shapes=[
+            pltpu.VMEM((HALF, PLANE), BF16),
+            pltpu.SemaphoreType.DMA((STORES + C * C // HALF,)),
+            pltpu.SemaphoreType.DMA((4, 2)),
+        ],
+        compiler_params=pltpu.CompilerParams(vmem_limit_bytes=6 * 2**20),
+    )(*(pltpu.with_memory_space_constraint(result, pltpu.VMEM) for result in results))
     return grad_fields.reshape(1, XD, C, PLANE), grad_weight
 
 

time: 69.4 us -> 68.1 us (0.981)
  Pallas kernels: 68.6 us -> 67.4 us
    pallas_call x2, Pallas kernels: 68.6 us -> 67.4 us  [the longest x1 65.7 us: per_device(): pl.pallas_call(kernel, out_shape=(pltpu.VMEM((HALF, PLANE), BF16), pltpu....]
where the time goes in v3:
time: 68.1 us; the launch traced here: 68 us
  Pallas kernels  67.4 us (99%)
    pallas_call x1, Pallas kernels, per_device(): pl.pallas_call(kernel, out_shape=(pltpu.VMEM((HALF, PLANE), BF16), pltpu....  65.7 us
    pallas_call x1, Pallas kernels, per_device(): pl.pallas_call(last_kernel, out_shape=(jax.ShapeDtypeStruct((ROWS, PLANE)...  1.68 us

profile of v3, /device:TPU:1, one launch (start us, length us, event | category | flops | bytes accessed | tf_op | source)
XLA Modules:
  0.0 68.0 jit_solution(795157339852306967)
XLA Ops:
  0.6 65.7 %shard_map.104 = (bf16[128,4096]{1,0:T(8,128)(2,1)S(1)}, f32[8,4,2,16,128]{4,3,2,1,0:T(8,128)S(1)}, bf16[512,2048]{1,0:T(8,128)(2,1)S(1)}, f32[256,2048]{1,0:T(8,128)S(1)}, bf16[128,512]{1,0:T(8,128)(2,1)S(1)}) custom-call(bf16[256,4096]{1,0:T(8,128)(2,1)} %bitcast.3, bf16[256,4096]{1,0:T(8,128)(2,1)} %bitcast.4, bf16[32,2,16,1024]{3,2,1,0:T(8,128)(2,1)} %w_hbm.1, ...), custom_call_target="tpu_custom_call" | custom-call | flops 5000000000 | bytes 16777216 | tf_op jit(solution)/shard_map/pallas_call | solution.py:591
  66.4 1.7 %shard_map.105 = (bf16[256,4096]{1,0:T(8,128)(2,1)}, f32[4,2,16,1024]{3,2,1,0:T(8,128)}) custom-call(bf16[128,4096]{1,0:T(8,128)(2,1)S(1)} %get-tuple-element.9.out_ref, f32[8,4,2,16,128]{4,3,2,1,0:T(8,128)S(1)} %get-tuple-element.10.gw_ref, bf16[512,2048]{1,0:T(8,128)(2,1)S(1)} %get-tuple-element.11.table_ref, f32[256,2048]{1,0:T(8,128)S(1)} %get-tuple-element.12.even_ref, ...), custom_call_target="tpu_custom_call" | custom-call | tf_op jit(solution)/shard_map/pallas_call | solution.py:647

commit v4 on v3

--- a/solution.py
+++ b/solution.py
@@ -130,7 +130,7 @@
     out_ref, gw_ref, odd_table, even, tail_ref,
     x_ref, cot_ref, w_ref, even_table, tw_ref, spread_ref, first_ref, gather_ref, parity_ref,
     send, recv, folded, weight, acc, spec, terms, mixed, dx, dg,
-    x_sem, table_sem, load_sem, own_sem, send_sem, recv_sem, dp_send, dp_recv, dp_own,
+    x_sem, table_sem, load_sem, own_sem, send_sem, recv_sem, dp_send, dp_recv, dp_own, ready_sem,
 ):
     table = (even_table, odd_table)
     me = lax.axis_index("pencil")
@@ -187,14 +187,16 @@
         )
         return carry
 
-    def greet_group(i, carry):
-        pl.semaphore_signal(
-            barrier, inc=1, device_id=(lax.rem(group + i, GROUPS), me), device_id_type=MESH
-        )
+    def greet_group(peer, carry):
+        pl.semaphore_signal(barrier, inc=1, device_id=(peer, me), device_id_type=MESH)
         return carry
 
+    def answer_group(peer, carry):
+        pl.semaphore_signal(ready_sem, inc=1, device_id=(peer, me), device_id_type=MESH)
+        return carry
+
     lax.fori_loop(1, PENCIL, greet_pencil, 0)
-    lax.fori_loop(1, GROUPS, greet_group, 0)
+    lax.fori_loop(group + 1, GROUPS, greet_group, 0)
 
     def block(ref, phase, parity, part, places):
         if part is None:
@@ -432,11 +434,12 @@
         load.start()
 
     def all_here():
-        pl.semaphore_wait(barrier, PENCIL + GROUPS - 2)
+        pl.semaphore_wait(barrier, PENCIL - 1 + group)
 
     plane_forward(folded[0], 0, 0, None, load_table, all_here)
     loads[0].wait()
     plane_forward(folded[1], 0, 1, None)
+    lax.fori_loop(0, group, answer_group, 0)
 
     loads[1].wait()
     loads[2].wait()
@@ -481,6 +484,11 @@
         odd_cells(1, half, slopes)
         for parity in range(2):
             plane_forward(folded[parity, pl.ds(half * HALF, HALF)], 2, parity, half)
+
+    @pl.when(group < GROUPS - 1)
+    def _():
+        pl.semaphore_wait(ready_sem, GROUPS - 1 - group)
+
     for parity in range(2):
         share(spec, dx, 0, parity)
 
@@ -498,6 +506,9 @@
                 post_all(3, parity, half)
         if parity == 0:
             post_all(3, parity, None)
+
+    arrived(3, 0, None)
+    even_cells(3, None)
 
     for parity in range(2):
         shared(spec, dx, 0, parity)
@@ -522,8 +533,7 @@
         return carry
 
     lax.fori_loop(0, MX // GROUPS, outer, 0, unroll=2)
-    arrived(3, 0, None)
-    even_cells(3, None)
+
 
     def finish(rows, near, far, one, two):
         out_ref[rows, near] = one.astype(BF16)
@@ -626,6 +636,7 @@
             pltpu.SemaphoreType.DMA((2, 2)),
             pltpu.SemaphoreType.DMA((2, 2)),
             pltpu.SemaphoreType.DMA((2, 2)),
+            pltpu.SemaphoreType.REGULAR,
         ],
         compiler_params=pltpu.CompilerParams(
             collective_id=0, has_side_effects=True, vmem_limit_bytes=48 * 2**20

time: 68.1 us -> 67.3 us (0.988)
  Pallas kernels: 67.4 us -> 66.4 us
    pallas_call x1, Pallas kernels: 65.7 us -> 64.7 us  [per_device(): pl.pallas_call(kernel, out_shape=(pltpu.VMEM((HALF, PLANE), BF16), pltpu....]
where the time goes in v4:
time: 67.3 us; the launch traced here: 67.2 us
  Pallas kernels  66.4 us (99%)
  between operations  0.8 us (1%)
    pallas_call x1, Pallas kernels, per_device(): pl.pallas_call(kernel, out_shape=(pltpu.VMEM((HALF, PLANE), BF16), pltpu....  64.7 us
    pallas_call x1, Pallas kernels, per_device(): pl.pallas_call(last_kernel, out_shape=(jax.ShapeDtypeStruct((ROWS, PLANE)...  1.68 us

profile of v4, /device:TPU:1, one launch (start us, length us, event | category | flops | bytes accessed | tf_op | source)
XLA Modules:
  0.0 67.2 jit_solution(14983109598918460683)
XLA Ops:
  0.6 64.7 %shard_map.104 = (bf16[128,4096]{1,0:T(8,128)(2,1)S(1)}, f32[8,4,2,16,128]{4,3,2,1,0:T(8,128)S(1)}, bf16[512,2048]{1,0:T(8,128)(2,1)S(1)}, f32[256,2048]{1,0:T(8,128)S(1)}, bf16[128,512]{1,0:T(8,128)(2,1)S(1)}) custom-call(bf16[256,4096]{1,0:T(8,128)(2,1)} %bitcast.3, bf16[256,4096]{1,0:T(8,128)(2,1)} %bitcast.4, bf16[32,2,16,1024]{3,2,1,0:T(8,128)(2,1)} %w_hbm.1, ...), custom_call_target="tpu_custom_call" | custom-call | flops 5000000000 | bytes 16777216 | tf_op jit(solution)/shard_map/pallas_call | solution.py:601
  65.3 1.7 %shard_map.105 = (bf16[256,4096]{1,0:T(8,128)(2,1)}, f32[4,2,16,1024]{3,2,1,0:T(8,128)}) custom-call(bf16[128,4096]{1,0:T(8,128)(2,1)S(1)} %get-tuple-element.9.out_ref, f32[8,4,2,16,128]{4,3,2,1,0:T(8,128)S(1)} %get-tuple-element.10.gw_ref, bf16[512,2048]{1,0:T(8,128)(2,1)S(1)} %get-tuple-element.11.table_ref, f32[256,2048]{1,0:T(8,128)S(1)} %get-tuple-element.12.even_ref, ...), custom_call_target="tpu_custom_call" | custom-call | tf_op jit(solution)/shard_map/pallas_call | solution.py:658

commit v5 on v4

--- a/solution.py
+++ b/solution.py
@@ -230,17 +230,19 @@
         whole = block(send, phase, parity, part, pl.ds(0, PENCIL - 1))
         pltpu.make_async_copy(whole, whole, send_sem.at[phase, parity, part or 0]).wait()
 
+    ring = [lax.rem(core + k, CORES) for k in range(CORES)]
+
     def post_stacks(phase, parity, part, steps):
-        def one(i, carry):
-            peer = stack_at(i // CORES) * CORES + lax.rem(core + i, CORES)
-
-            @pl.when(peer != me)
-            def _():
-                post(phase, parity, part, peer)
-
+        def one(step, carry):
+            base = stack_at(step) * CORES
+            for place in ring:
+                post(phase, parity, part, base + place)
             return carry
 
-        lax.fori_loop(steps[0] * CORES, steps[1] * CORES, one, 0)
+        lax.fori_loop(steps[0], min(steps[1], STACKS - 1), one, 0)
+        if steps[1] == STACKS:
+            for place in ring[1:]:
+                post(phase, parity, part, stack * CORES + place)
 
     def post_all(phase, parity, part):
         post_stacks(phase, parity, part, (0, STACKS))

time: 67.3 us -> 65.9 us (0.979)
  Pallas kernels: 66.4 us -> 65 us
    pallas_call x1, Pallas kernels: 64.7 us -> 63.4 us  [per_device(): pl.pallas_call(kernel, out_shape=(pltpu.VMEM((HALF, PLANE), BF16), pltpu....]
where the time goes in v5:
time: 65.9 us; the launch traced here: 65.8 us
  Pallas kernels  65 us (99%)
  between operations  0.8 us (1%)
    pallas_call x1, Pallas kernels, per_device(): pl.pallas_call(kernel, out_shape=(pltpu.VMEM((HALF, PLANE), BF16), pltpu....  63.4 us
    pallas_call x1, Pallas kernels, per_device(): pl.pallas_call(last_kernel, out_shape=(jax.ShapeDtypeStruct((ROWS, PLANE)...  1.68 us

profile of v5, /device:TPU:1, one launch (start us, length us, event | category | flops | bytes accessed | tf_op | source)
XLA Modules:
  0.0 65.8 jit_solution(15443145265041612292)
XLA Ops:
  0.6 63.4 %shard_map.104 = (bf16[128,4096]{1,0:T(8,128)(2,1)S(1)}, f32[8,4,2,16,128]{4,3,2,1,0:T(8,128)S(1)}, bf16[512,2048]{1,0:T(8,128)(2,1)S(1)}, f32[256,2048]{1,0:T(8,128)S(1)}, bf16[128,512]{1,0:T(8,128)(2,1)S(1)}) custom-call(bf16[256,4096]{1,0:T(8,128)(2,1)} %bitcast.3, bf16[256,4096]{1,0:T(8,128)(2,1)} %bitcast.4, bf16[32,2,16,1024]{3,2,1,0:T(8,128)(2,1)} %w_hbm.1, ...), custom_call_target="tpu_custom_call" | custom-call | flops 5000000000 | bytes 16777216 | tf_op jit(solution)/shard_map/pallas_call | solution.py:603
  64.0 1.7 %shard_map.105 = (bf16[256,4096]{1,0:T(8,128)(2,1)}, f32[4,2,16,1024]{3,2,1,0:T(8,128)}) custom-call(bf16[128,4096]{1,0:T(8,128)(2,1)S(1)} %get-tuple-element.9.out_ref, f32[8,4,2,16,128]{4,3,2,1,0:T(8,128)S(1)} %get-tuple-element.10.gw_ref, bf16[512,2048]{1,0:T(8,128)(2,1)S(1)} %get-tuple-element.11.table_ref, f32[256,2048]{1,0:T(8,128)S(1)} %get-tuple-element.12.even_ref, ...), custom_call_target="tpu_custom_call" | custom-call | tf_op jit(solution)/shard_map/pallas_call | solution.py:660
